TPU v7x, 32 devices: a whole 2x2x4 slice. The times are simulated.
32 devices in a mesh: blk: 8 (over z, y), lag: 4 (over x, core).
Axes of the slice: x: 2, y: 2, z: 4, core: 2. Of those that a mesh axis runs over, the one named last changes fastest.
Arguments:
- seismograms: float32 [1024, 3, 1024], P(('blk', 'lag')), may hold values from -70 to 70
- onset_shift: int32 [1024], P(('blk', 'lag')), may hold values from 0 to 63
- start_bits: int32 [1024], P(('blk', 'lag')), may hold values from 0 to 65535
Outputs:
- embedding: float32 [16, 1024], P(None, ('blk', 'lag'))
Inputs may be any that keep to these rules, and one draw needn't show every extreme that they name: `start_bits`: bit k of an event's code is its entry in starting vector k.
All inputs are finite; a program needn't handle non-finite values.
Results may differ from a plain program's by a relative error of at most 0.0077.
Values may be sent and summed in bfloat16 or wider, within the bound.
A program may use at most 64 MiB of HBM per device.

v0:
```python
import jax
import jax.numpy as jnp
from jax import lax
from jax.sharding import PartitionSpec as P

SAMPLES = 1024
MAXLAG = 64
LAGS = 65
OFFMAX = 64
VECTORS = 16
ITERS = 3
sharpness = 64.0


def passed_along(value, axis, steps):
    count = lax.axis_size(axis)
    pairs = [(source, (source + steps) % count) for source in range(count)]
    return lax.ppermute(value, axis, pairs)


def align_unit(seismograms, onset_shift):
    padded = jnp.pad(seismograms, ((0, 0), (0, 0), (0, OFFMAX)))

    def slide(record, offset_at):
        return lax.dynamic_slice_in_dim(record, offset_at, SAMPLES, 1)

    aligned = jax.vmap(slide)(padded, onset_shift)
    energy = jnp.sum(aligned * aligned, axis=(1, 2))
    return (aligned * lax.rsqrt(energy + 1e-06)[:, None, None]).astype(jnp.bfloat16)


def neighbour_waves(unit_waves):
    centre = lax.all_gather(unit_waves, "lag", axis=0, tiled=True)
    beyond = passed_along(centre, "blk", -1)
    before = passed_along(centre, "blk", 1)
    blocks = (before, centre, beyond)
    return blocks


def neighbour_vectors(scaled):
    centre = lax.all_gather(scaled, "lag", axis=1, tiled=True)
    before = passed_along(centre, "blk", 1)
    beyond = passed_along(centre, "blk", -1)
    return jnp.concatenate((before, centre, beyond), 1)


def band_affinity(unit_waves, blocks):
    own_count = unit_waves.shape[0]
    flat_width = unit_waves.shape[1] * unit_waves.shape[2]
    padded = jnp.pad(unit_waves, ((0, 0), (0, 0), (MAXLAG, MAXLAG)))
    lag_group = 5
    flattened = [block.reshape(block.shape[0], flat_width) for block in blocks]

    def one_group(runnings, first_lag):
        shifted = jnp.concatenate(
            [
                lax.dynamic_slice_in_dim(
                    padded, 2 * MAXLAG - 2 * (first_lag + offset), SAMPLES, 2
                ).reshape(own_count, flat_width)
                for offset in range(lag_group)
            ],
            0,
        )
        updated = []
        for running, columns in zip(runnings, flattened):
            scores = lax.dot_general(
                shifted, columns, (((1,), (1,)), ((), ())), preferred_element_type=jnp.float32
            )
            weights = jnp.exp(sharpness * scores).reshape(lag_group, own_count, columns.shape[0])
            updated.append(running + jnp.sum(weights, axis=0))
        return (tuple(updated), None)

    starting = tuple(
        (jnp.zeros((own_count, columns.shape[0]), jnp.float32) for columns in flattened)
    )
    runnings, unused = lax.scan(
        one_group, starting, jnp.arange(0, LAGS, lag_group, dtype=jnp.int32)
    )
    return jnp.concatenate(runnings, 1)


def local(seismograms, onset_shift, start_bits):
    own_count = seismograms.shape[0]
    highest = lax.Precision.HIGHEST
    unit_waves = align_unit(seismograms, onset_shift)
    blocks = neighbour_waves(unit_waves)
    affinity = band_affinity(unit_waves, blocks)
    block_length = affinity.shape[1] // 3
    member = lax.axis_index("lag")
    column_ids = jnp.arange(3 * block_length, dtype=jnp.int32)
    self_ids = block_length + member * own_count + jnp.arange(own_count, dtype=jnp.int32)
    affinity = jnp.where(
        column_ids[None, :] == self_ids[:, None], jnp.zeros_like(affinity), affinity
    )
    degree = jnp.sum(affinity, axis=1)
    root_degree = jnp.sqrt(degree)
    inverse = lax.rsqrt(degree)
    events_all = own_count * lax.axis_size("blk") * lax.axis_size("lag")
    powers = 2 ** jnp.arange(VECTORS, dtype=jnp.int32)
    vectors = (start_bits[None, :] // powers[:, None] % 2).astype(jnp.float32)
    degree_total, projection = lax.psum(
        (jnp.sum(degree), jnp.dot(vectors, root_degree, precision=highest)), ("blk", "lag")
    )
    for iteration in range(ITERS):
        neighbours = neighbour_vectors(vectors * inverse)
        applied = lax.dot_general(neighbours, affinity, (((1,), (1,)), ((), ())), precision=highest)
        deflated = applied * inverse - root_degree * (projection / degree_total)[:, None]
        gram_local = jnp.dot(deflated, deflated.T, precision=highest)
        carried_local = jnp.dot(deflated, root_degree, precision=highest)
        gram_sum, carried = lax.psum((gram_local, carried_local), ("blk", "lag"))
        factor = jnp.linalg.cholesky(gram_sum / events_all)
        vectors = lax.linalg.triangular_solve(factor, deflated, left_side=True, lower=True)
        projection = lax.linalg.triangular_solve(
            factor, carried[:, None], left_side=True, lower=True
        )[:, 0]
    return vectors


def solution(mesh):
    return jax.shard_map(
        local,
        mesh=mesh,
        in_specs=(P(("blk", "lag"), None, None), P(("blk", "lag")), P(("blk", "lag"))),
        out_specs=P(None, ("blk", "lag")),
        check_vma=False,
    )
```

profile of v0, /device:TPU:10, one launch (start us, length us, event | category | flops | bytes accessed | tf_op | source)
XLA Modules:
  0.0 432.6 jit_solution(3291205660569676358)
XLA Ops:
  2.1 64.4 %while.19 = (s32[]{:T(128)}, f32[32,3,1088]{2,1,0:T(4,128)S(1)}, s32[32,3]{0,1:T(4,128)S(1)}, f32[32,3,1024]{2,1,0:T(4,128)S(1)}, s32[]{:T(128)}) while((s32[]{:T(128)}, f32[32,3,1088]{2,1,0:T(4,128)S(1)}, s32[32,3]{0,1:T(4,128)S(1)}, f32[32,3,1024]{2,1,0:T(4,128)S(1)}, s32[]{:T(128)}) %tuple.64), condition=%wide.while_cond, body=%wide.while_body.sunk | while | flops 2 | bytes 32893 | solution.py:25
  67.1 8.2 %all_gather.12 = bf16[128,3,1024]{2,0,1:T(8,128)(2,1)S(1)} all-gather(bf16[32,3,1024]{2,0,1:T(8,128)(2,1)S(1)} %fusion.12), channel_id=1, replica_groups=mesh['blk'=8,'lag'=4] {'lag'}, dimensions={0}, use_global_device_ids=true | all-gather | bytes 983040 | tf_op jit(solution)/shard_map/all_gather | solution.py:33
  75.6 1.5 collective-permute-start.1
  79.1 33.3 %collective-permute-done.1 = bf16[128,3,1024]{0,2,1:T(8,128)(2,1)} collective-permute-done((bf16[128,3,1024]{0,2,1:T(8,128)(2,1)S(1)}, bf16[128,3,1024]{0,2,1:T(8,128)(2,1)}, u32[]{:S(2)}, u32[]{:S(2)}) %collective-permute-start.1) | collective-permute-done | bytes 786464 | tf_op jit(solution)/shard_map/ppermute | solution.py:18
  115.0 103.0 %while.20 = (s32[]{:T(128)}, f32[32,128]{1,0:T(8,128)S(1)}, f32[32,128]{1,0:T(8,128)S(1)}, f32[32,128]{1,0:T(8,128)S(1)}, s32[13]{0:T(128)S(1)}, /*index=5*/bf16...) while((s32[]{:T(128)}, f32[32,128]{1,0:T(8,128)S(1)}, ...), condition=%wide.region_5.6_spmd.clone, body=%wide.region_1.5_spmd.clone.sunk | while | flops 377622560 | bytes 15041106 | solution.py:76
  118.9 1.4 constant_dynamic-slice_fusion.9
  150.6 1.4 constant_dynamic-slice_fusion.9
  166.4 1.4 constant_dynamic-slice_fusion.9
  182.3 1.4 constant_dynamic-slice_fusion.9
  198.1 1.4 constant_dynamic-slice_fusion.9
  214.0 1.4 constant_dynamic-slice_fusion.9
  219.3 5.2 %all-gather = f32[4,32,16]{1,2,0:T(8,128)S(1)} all-gather(f32[1,32,16]{1,2,0:T(8,128)S(1)} %multiply_bitcast_fusion), channel_id=1, replica_groups=mesh['blk'=8,'lag'=4] {'lag'}, dimensions={0}, use_global_device_ids=true | all-gather | bytes 10240 | tf_op jit(solution)/shard_map/all_gather | solution.py:41
  226.6 42.9 %all-reduce.5 = (f32[16]{0:T(128)S(1)}, f32[]{:T(128)}) all-reduce(f32[16]{0:T(128)S(1)} %convolution_bitcast_fusion.4, f32[]{:T(128)} %get-tuple-element.209), channel_id=1, replica_groups=mesh['blk'=8,'lag'=4] {'blk','lag'}, use_global_device_ids=true, to_apply=%region_7.8 | all-reduce | flops 17 | bytes 136 | tf_op jit(solution)/shard_map/psum | solution.py:101
  270.7 39.1 %all-reduce.4 = (f32[16,16]{0,1:T(8,128)S(1)}, f32[16,1]{0,1:T(1,128)S(1)}) all-reduce(f32[16,16]{0,1:T(8,128)S(1)} %fusion.69, f32[16,1]{0,1:T(1,128)S(1)} %convolution_bitcast_fusion.3), channel_id=1, replica_groups=mesh['blk'=8,'lag'=4] {'blk','lag'}, use_global_device_ids=true, to_apply=%region_10.11 | all-reduce | flops 272 | bytes 2176 | tf_op jit(solution)/shard_map/psum | solution.py:110
  309.9 1.5 cholesky.59
  314.2 5.2 %all-gather.1 = f32[4,32,16]{1,2,0:T(8,128)S(1)} all-gather(f32[1,32,16]{1,2,0:T(8,128)S(1)} %fusion.6), channel_id=1, replica_groups=mesh['blk'=8,'lag'=4] {'lag'}, dimensions={0}, use_global_device_ids=true | all-gather | bytes 10240 | tf_op jit(solution)/shard_map/all_gather | solution.py:41
  319.5 2.7 collective-permute-start.5
  323.6 3.2 collective-permute-done.4
  327.3 43.0 %all-reduce.3 = (f32[16,16]{0,1:T(8,128)S(1)}, f32[16,1]{0,1:T(1,128)S(1)}) all-reduce(f32[16,16]{0,1:T(8,128)S(1)} %fusion.70, f32[16,1]{0,1:T(1,128)S(1)} %convolution_bitcast_fusion.1), channel_id=1, replica_groups=mesh['blk'=8,'lag'=4] {'blk','lag'}, use_global_device_ids=true, to_apply=%region_14.18 | all-reduce | flops 272 | bytes 2176 | tf_op jit(solution)/shard_map/psum | solution.py:110
  370.4 1.5 cholesky.70
  374.7 5.2 %all-gather.2 = f32[4,32,16]{1,2,0:T(8,128)S(1)} all-gather(f32[1,32,16]{1,2,0:T(8,128)S(1)} %fusion.4), channel_id=1, replica_groups=mesh['blk'=8,'lag'=4] {'lag'}, dimensions={0}, use_global_device_ids=true | all-gather | bytes 10240 | tf_op jit(solution)/shard_map/all_gather | solution.py:41
  380.0 2.0 collective-permute-start.6
  385.0 42.7 %psum.55 = f32[16,16]{0,1:T(8,128)S(1)} all-reduce(f32[16,16]{0,1:T(8,128)S(1)} %fusion.71), channel_id=1, replica_groups=mesh['blk'=8,'lag'=4] {'blk','lag'}, use_global_device_ids=true, to_apply=%region_16.20 | all-reduce | flops 256 | bytes 2048 | tf_op jit(solution)/shard_map/psum | solution.py:110
  427.7 1.5 cholesky.81
  (458 shorter events, 141.7 us)
Async XLA Ops:
  0.0 0.7 copy-start.2
  75.6 36.8 %collective-permute-start.1 = (bf16[128,3,1024]{0,2,1:T(8,128)(2,1)S(1)}, bf16[128,3,1024]{0,2,1:T(8,128)(2,1)}, u32[]{:S(2)}, u32[]{:S(2)}) collective-permute-start(bf16[128,3,1024]{0,2,1:T(8,128)(2,1)S(1)} %copy.28), channel_id=1, source_target_pairs={{0,28},{4,0},{8,4},{12,8},{16,12},{20,16},{24,20},{28,24},{1,29},{... | collective-permute-start | bytes 2359304 | tf_op jit(solution)/shard_map/ppermute | solution.py:18
  77.1 36.8 %collective-permute-start = (bf16[128,3,1024]{0,2,1:T(8,128)(2,1)S(1)}, bf16[128,3,1024]{0,2,1:T(8,128)(2,1)S(1)}, u32[]{:S(2)}, u32[]{:S(2)}) collective-permute-start(bf16[128,3,1024]{0,2,1:T(8,128)(2,1)S(1)} %copy.28), channel_id=1, source_target_pairs={{0,4},{4,8},{8,12},{12,16},{16,20},{20,24},{24,28},{28,0},{1,5},{5... | collective-permute-start | bytes 2359304 | tf_op jit(solution)/shard_map/ppermute | solution.py:18
  77.9 0.7 copy-start.1
  121.3 1.1 copy-start
  129.2 1.1 copy-start
  137.2 1.1 copy-start
  145.1 1.1 copy-start
  153.0 1.1 copy-start
  160.9 1.1 copy-start
  168.9 1.1 copy-start
  176.8 1.1 copy-start
  184.7 1.1 copy-start
  192.6 1.1 copy-start
  200.6 1.1 copy-start
  208.5 1.1 copy-start
  216.4 1.1 copy-start
  224.6 45.6 %collective-permute-start.3 = (f32[16,128]{1,0:T(8,128)S(1)}, f32[16,128]{1,0:T(8,128)S(1)}, u32[]{:S(2)}, u32[]{:S(2)}) collective-permute-start(f32[16,128]{1,0:T(8,128)S(1)} %bitcast.222), channel_id=1, source_target_pairs={{0,28},{4,0},{8,4},{12,8},{16,12},{20,16},{24,20},{28,24},{1,29},{... | collective-permute-start | bytes 24584 | tf_op jit(solution)/shard_map/ppermute | solution.py:18
  225.4 44.7 %collective-permute-start.2 = (f32[16,128]{1,0:T(8,128)S(1)}, f32[16,128]{1,0:T(8,128)S(1)}, u32[]{:S(2)}, u32[]{:S(2)}) collective-permute-start(f32[16,128]{1,0:T(8,128)S(1)} %bitcast.223), channel_id=1, source_target_pairs={{0,4},{4,8},{8,12},{12,16},{16,20},{20,24},{24,28},{28,0},{1,5},{5... | collective-permute-start | bytes 24584 | tf_op jit(solution)/shard_map/ppermute | solution.py:18
  319.5 4.1 collective-permute-start.5
  322.2 4.5 %collective-permute-start.4 = (f32[16,128]{1,0:T(8,128)S(1)}, f32[16,128]{1,0:T(8,128)S(1)}, u32[]{:S(2)}, u32[]{:S(2)}) collective-permute-start(f32[16,128]{1,0:T(8,128)S(1)} %bitcast.226), channel_id=1, source_target_pairs={{0,4},{4,8},{8,12},{12,16},{16,20},{20,24},{24,28},{28,0},{1,5},{5... | collective-permute-start | bytes 24584 | tf_op jit(solution)/shard_map/ppermute | solution.py:18
  380.0 3.7 collective-permute-start.7
  380.0 4.6 %collective-permute-start.6 = (f32[16,128]{1,0:T(8,128)S(1)}, f32[16,128]{1,0:T(8,128)S(1)}, u32[]{:S(2)}, u32[]{:S(2)}) collective-permute-start(f32[16,128]{1,0:T(8,128)S(1)} %bitcast.220), channel_id=1, source_target_pairs={{0,4},{4,8},{8,12},{12,16},{16,20},{20,24},{24,28},{28,0},{1,5},{5... | collective-permute-start | bytes 24584 | tf_op jit(solution)/shard_map/ppermute | solution.py:18
where the time goes:
time: 435 us; the launch traced here: 433 us
  blocking collectives  191 us (44%)
  local copies, waits for them, and re-layouts  114 us (26%)
  loops' own time  43.5 us (10%)
  waiting for transfers between devices  38.9 us (9%)
  matrix products  21 us (5%)
  other arithmetic  15.1 us (3%)
  starting transfers between devices  8.82 us (2%)
    psum x3, blocking collectives, local(): gram_sum, carried = lax.psum((gram_local, carried_local), ('blk', 'lag'))  125 us
    gather x96, local copies, waits for them, and re-layouts  64.4 us
    another operation x1, loops' own time, band_affinity(): lax.scan(one_group, starting, jnp.arange(0, LAGS, lag_group, dtype=jnp.in...  43.5 us
    psum x1, blocking collectives, local(): lax.psum((jnp.sum(degree), jnp.dot(vectors, root_degree, precision=highes...  42.9 us
    ppermute x8, waiting for transfers between devices, passed_along(): return lax.ppermute(value, axis, pairs)  38.9 us
    dynamic_slice x13, local copies, waits for them, and re-layouts, one_group(): lax.dynamic_slice_in_dim(padded, 2 * MAXLAG - 2 * (first_lag + offset), S...  18.6 us
    dot_general x39, matrix products, one_group(): lax.dot_general(shifted, columns, (((1,), (1,)), ((), ())), preferred_ele...  16.5 us
    all_gather x3, blocking collectives, neighbour_vectors(): centre = lax.all_gather(scaled, 'lag', axis=1, tiled=True)  15.6 us
  transfers between devices with their start and end apart: 8, of which 5 were waited for; matrix products, arithmetic and copies ran while one was open for 1% of the time, Pallas kernels for 0%

commit v1 on v0

--- a/solution.py
+++ b/solution.py
@@ -107,7 +107,7 @@
         deflated = applied * inverse - root_degree * (projection / degree_total)[:, None]
         gram_local = jnp.dot(deflated, deflated.T, precision=highest)
         carried_local = jnp.dot(deflated, root_degree, precision=highest)
-        gram_sum, carried = lax.psum((gram_local, carried_local), ("blk", "lag"))
+        gram_sum, carried = lax.psum(lax.psum((gram_local, carried_local), "lag"), "blk")
         factor = jnp.linalg.cholesky(gram_sum / events_all)
         vectors = lax.linalg.triangular_solve(factor, deflated, left_side=True, lower=True)
         projection = lax.linalg.triangular_solve(

time: 435 us -> 387 us (0.89); the launches traced: 433 us -> 380 us
  blocking collectives: 191 us -> 134 us
    psum x3 -> x6, blocking collectives: 125 us -> 67.1 us  [the longest x3 49.3 us: local(): lax.psum(lax.psum((gram_local, carried_local), 'lag'), 'blk')]
where the time goes in v1:
time: 387 us; the launch traced here: 380 us
  blocking collectives  134 us (35%)
  local copies, waits for them, and re-layouts  114 us (29%)
  loops' own time  43.5 us (11%)
  waiting for transfers between devices  40.9 us (11%)
  matrix products  21 us (5%)
  other arithmetic  15.1 us (4%)
  starting transfers between devices  11.6 us (3%)
    gather x96, local copies, waits for them, and re-layouts  64.4 us
    psum x3, blocking collectives, local(): lax.psum(lax.psum((gram_local, carried_local), 'lag'), 'blk')  49.3 us
    another operation x1, loops' own time, band_affinity(): lax.scan(one_group, starting, jnp.arange(0, LAGS, lag_group, dtype=jnp.in...  43.5 us
    psum x1, blocking collectives, local(): lax.psum((jnp.sum(degree), jnp.dot(vectors, root_degree, precision=highes...  42.9 us
    ppermute x8, waiting for transfers between devices, passed_along(): return lax.ppermute(value, axis, pairs)  40.9 us
    dynamic_slice x13, local copies, waits for them, and re-layouts, one_group(): lax.dynamic_slice_in_dim(padded, 2 * MAXLAG - 2 * (first_lag + offset), S...  18.6 us
    psum x3, blocking collectives, local(): lax.psum((gram_local, carried_local), 'lag')  17.8 us
    dot_general x39, matrix products, one_group(): lax.dot_general(shifted, columns, (((1,), (1,)), ((), ())), preferred_ele...  16.5 us
  transfers between devices with their start and end apart: 8, of which 5 were waited for; matrix products, arithmetic and copies ran while one was open for 1% of the time, Pallas kernels for 0%

profile of v1, /device:TPU:10, one launch (start us, length us, event | category | flops | bytes accessed | tf_op | source)
XLA Modules:
  0.0 379.8 jit_solution(11786947263786105502)
XLA Ops:
  2.1 64.4 %while.19 = (s32[]{:T(128)}, f32[32,3,1088]{2,1,0:T(4,128)S(1)}, s32[32,3]{0,1:T(4,128)S(1)}, f32[32,3,1024]{2,1,0:T(4,128)S(1)}, s32[]{:T(128)}) while((s32[]{:T(128)}, f32[32,3,1088]{2,1,0:T(4,128)S(1)}, s32[32,3]{0,1:T(4,128)S(1)}, f32[32,3,1024]{2,1,0:T(4,128)S(1)}, s32[]{:T(128)}) %tuple.64), condition=%wide.while_cond, body=%wide.while_body.sunk | while | flops 2 | bytes 32893 | solution.py:25
  67.1 8.2 %all_gather.12 = bf16[128,3,1024]{2,0,1:T(8,128)(2,1)S(1)} all-gather(bf16[32,3,1024]{2,0,1:T(8,128)(2,1)S(1)} %fusion.12), channel_id=1, replica_groups=mesh['blk'=8,'lag'=4] {'lag'}, dimensions={0}, use_global_device_ids=true | all-gather | bytes 983040 | tf_op jit(solution)/shard_map/all_gather | solution.py:33
  75.6 1.5 collective-permute-start.1
  79.1 33.3 %collective-permute-done.1 = bf16[128,3,1024]{0,2,1:T(8,128)(2,1)} collective-permute-done((bf16[128,3,1024]{0,2,1:T(8,128)(2,1)S(1)}, bf16[128,3,1024]{0,2,1:T(8,128)(2,1)}, u32[]{:S(2)}, u32[]{:S(2)}) %collective-permute-start.1) | collective-permute-done | bytes 786464 | tf_op jit(solution)/shard_map/ppermute | solution.py:18
  115.0 103.0 %while.20 = (s32[]{:T(128)}, f32[32,128]{1,0:T(8,128)S(1)}, f32[32,128]{1,0:T(8,128)S(1)}, f32[32,128]{1,0:T(8,128)S(1)}, s32[13]{0:T(128)S(1)}, /*index=5*/bf16...) while((s32[]{:T(128)}, f32[32,128]{1,0:T(8,128)S(1)}, ...), condition=%wide.region_5.6_spmd.clone, body=%wide.region_1.5_spmd.clone.sunk | while | flops 377622560 | bytes 15041106 | solution.py:76
  118.9 1.4 constant_dynamic-slice_fusion.9
  150.6 1.4 constant_dynamic-slice_fusion.9
  219.3 5.2 %all-gather = f32[4,32,16]{1,2,0:T(8,128)S(1)} all-gather(f32[1,32,16]{1,2,0:T(8,128)S(1)} %multiply_bitcast_fusion), channel_id=1, replica_groups=mesh['blk'=8,'lag'=4] {'lag'}, dimensions={0}, use_global_device_ids=true | all-gather | bytes 10240 | tf_op jit(solution)/shard_map/all_gather | solution.py:41
  226.6 42.9 %all-reduce.3 = (f32[16]{0:T(128)S(1)}, f32[]{:T(128)}) all-reduce(f32[16]{0:T(128)S(1)} %convolution_bitcast_fusion.4, f32[]{:T(128)} %get-tuple-element.209), channel_id=1, replica_groups=mesh['blk'=8,'lag'=4] {'blk','lag'}, use_global_device_ids=true, to_apply=%region_7.8 | all-reduce | flops 17 | bytes 136 | tf_op jit(solution)/shard_map/psum | solution.py:101
  270.7 6.0 %all-reduce.7 = (f32[16,16]{0,1:T(8,128)S(1)}, f32[16]{0:T(128)S(1)}) all-reduce(f32[16,16]{0,1:T(8,128)S(1)} %fusion.69, f32[16]{0:T(128)S(1)} %convolution_bitcast_fusion.3), channel_id=1, replica_groups=mesh['blk'=8,'lag'=4] {'lag'}, use_global_device_ids=true, to_apply=%region_10.11 | all-reduce | flops 272 | bytes 2176 | tf_op jit(solution)/shard_map/psum | solution.py:110
  276.7 16.2 %all-reduce.5 = (f32[16,16]{0,1:T(8,128)S(1)}, f32[16,1]{0,1:T(1,128)S(1)}) all-reduce(f32[16,16]{0,1:T(8,128)S(1)} %get-tuple-element.245, f32[16,1]{0,1:T(1,128)S(1)} %bitcast.228), channel_id=1, replica_groups=mesh['blk'=8,'lag'=4] {'blk'}, use_global_device_ids=true, to_apply=%region_11.12 | all-reduce | flops 272 | bytes 2176 | tf_op jit(solution)/shard_map/psum | solution.py:110
  293.0 1.5 cholesky.59
  297.4 5.2 %all-gather.1 = f32[4,32,16]{1,2,0:T(8,128)S(1)} all-gather(f32[1,32,16]{1,2,0:T(8,128)S(1)} %fusion.6), channel_id=1, replica_groups=mesh['blk'=8,'lag'=4] {'lag'}, dimensions={0}, use_global_device_ids=true | all-gather | bytes 10240 | tf_op jit(solution)/shard_map/all_gather | solution.py:41
  302.7 2.8 collective-permute-start.5
  306.8 3.2 collective-permute-done.4
  310.5 6.0 %all-reduce.6 = (f32[16,16]{0,1:T(8,128)S(1)}, f32[16]{0:T(128)S(1)}) all-reduce(f32[16,16]{0,1:T(8,128)S(1)} %fusion.70, f32[16]{0:T(128)S(1)} %convolution_bitcast_fusion.1), channel_id=1, replica_groups=mesh['blk'=8,'lag'=4] {'lag'}, use_global_device_ids=true, to_apply=%region_16.20 | all-reduce | flops 272 | bytes 2176 | tf_op jit(solution)/shard_map/psum | solution.py:110
  316.6 16.6 %all-reduce.4 = (f32[16,16]{0,1:T(8,128)S(1)}, f32[16,1]{0,1:T(1,128)S(1)}) all-reduce(f32[16,16]{0,1:T(8,128)S(1)} %get-tuple-element.243, f32[16,1]{0,1:T(1,128)S(1)} %bitcast.229), channel_id=1, replica_groups=mesh['blk'=8,'lag'=4] {'blk'}, use_global_device_ids=true, to_apply=%region_17.21 | all-reduce | flops 272 | bytes 2176 | tf_op jit(solution)/shard_map/psum | solution.py:110
  333.3 1.5 cholesky.70
  337.6 5.2 %all-gather.2 = f32[4,32,16]{1,2,0:T(8,128)S(1)} all-gather(f32[1,32,16]{1,2,0:T(8,128)S(1)} %fusion.4), channel_id=1, replica_groups=mesh['blk'=8,'lag'=4] {'lag'}, dimensions={0}, use_global_device_ids=true | all-gather | bytes 10240 | tf_op jit(solution)/shard_map/all_gather | solution.py:41
  342.9 4.7 %collective-permute-start.7 = (f32[16,128]{1,0:T(8,128)S(1)}, f32[16,128]{1,0:T(8,128)S(1)}, u32[]{:S(2)}, u32[]{:S(2)}) collective-permute-start(f32[16,128]{1,0:T(8,128)S(1)} %bitcast.219), channel_id=1, source_target_pairs={{0,28},{4,0},{8,4},{12,8},{16,12},{20,16},{24,20},{28,24},{1,29},{... | collective-permute-start | bytes 24584 | tf_op jit(solution)/shard_map/ppermute | solution.py:18
  349.0 3.2 collective-permute-done.6
  352.5 5.8 %psum.94 = f32[16,16]{0,1:T(8,128)S(1)} all-reduce(f32[16,16]{0,1:T(8,128)S(1)} %fusion.71), channel_id=1, replica_groups=mesh['blk'=8,'lag'=4] {'lag'}, use_global_device_ids=true, to_apply=%region_20.24 | all-reduce | flops 256 | bytes 2048 | tf_op jit(solution)/shard_map/psum | solution.py:110
  358.3 16.5 %psum.95 = f32[16,16]{0,1:T(8,128)S(1)} all-reduce(f32[16,16]{0,1:T(8,128)S(1)} %psum.94), channel_id=1, replica_groups=mesh['blk'=8,'lag'=4] {'blk'}, use_global_device_ids=true, to_apply=%region_21.25 | all-reduce | flops 256 | bytes 2048 | tf_op jit(solution)/shard_map/psum | solution.py:110
  374.9 1.5 cholesky.81
  (461 shorter events, 146.2 us)
Async XLA Ops:
  0.0 0.7 copy-start.2
  75.6 36.8 %collective-permute-start.1 = (bf16[128,3,1024]{0,2,1:T(8,128)(2,1)S(1)}, bf16[128,3,1024]{0,2,1:T(8,128)(2,1)}, u32[]{:S(2)}, u32[]{:S(2)}) collective-permute-start(bf16[128,3,1024]{0,2,1:T(8,128)(2,1)S(1)} %copy.28), channel_id=1, source_target_pairs={{0,28},{4,0},{8,4},{12,8},{16,12},{20,16},{24,20},{28,24},{1,29},{... | collective-permute-start | bytes 2359304 | tf_op jit(solution)/shard_map/ppermute | solution.py:18
  77.1 36.8 %collective-permute-start = (bf16[128,3,1024]{0,2,1:T(8,128)(2,1)S(1)}, bf16[128,3,1024]{0,2,1:T(8,128)(2,1)S(1)}, u32[]{:S(2)}, u32[]{:S(2)}) collective-permute-start(bf16[128,3,1024]{0,2,1:T(8,128)(2,1)S(1)} %copy.28), channel_id=1, source_target_pairs={{0,4},{4,8},{8,12},{12,16},{16,20},{20,24},{24,28},{28,0},{1,5},{5... | collective-permute-start | bytes 2359304 | tf_op jit(solution)/shard_map/ppermute | solution.py:18
  77.9 0.7 copy-start.1
  121.3 1.1 copy-start
  129.2 1.1 copy-start
  137.2 1.1 copy-start
  145.1 1.1 copy-start
  153.0 1.1 copy-start
  160.9 1.1 copy-start
  168.9 1.1 copy-start
  176.8 1.1 copy-start
  184.7 1.1 copy-start
  192.6 1.1 copy-start
  200.6 1.1 copy-start
  208.5 1.1 copy-start
  216.4 1.1 copy-start
  224.6 45.6 %collective-permute-start.3 = (f32[16,128]{1,0:T(8,128)S(1)}, f32[16,128]{1,0:T(8,128)S(1)}, u32[]{:S(2)}, u32[]{:S(2)}) collective-permute-start(f32[16,128]{1,0:T(8,128)S(1)} %bitcast.222), channel_id=1, source_target_pairs={{0,28},{4,0},{8,4},{12,8},{16,12},{20,16},{24,20},{28,24},{1,29},{... | collective-permute-start | bytes 24584 | tf_op jit(solution)/shard_map/ppermute | solution.py:18
  225.4 44.7 %collective-permute-start.2 = (f32[16,128]{1,0:T(8,128)S(1)}, f32[16,128]{1,0:T(8,128)S(1)}, u32[]{:S(2)}, u32[]{:S(2)}) collective-permute-start(f32[16,128]{1,0:T(8,128)S(1)} %bitcast.223), channel_id=1, source_target_pairs={{0,4},{4,8},{8,12},{12,16},{16,20},{20,24},{24,28},{28,0},{1,5},{5... | collective-permute-start | bytes 24584 | tf_op jit(solution)/shard_map/ppermute | solution.py:18
  302.7 4.2 %collective-permute-start.5 = (f32[16,128]{1,0:T(8,128)S(1)}, f32[16,128]{1,0:T(8,128)S(1)}, u32[]{:S(2)}, u32[]{:S(2)}) collective-permute-start(f32[16,128]{1,0:T(8,128)S(1)} %bitcast.225), channel_id=1, source_target_pairs={{0,28},{4,0},{8,4},{12,8},{16,12},{20,16},{24,20},{28,24},{1,29},{... | collective-permute-start | bytes 24584 | tf_op jit(solution)/shard_map/ppermute | solution.py:18
  305.5 4.5 %collective-permute-start.4 = (f32[16,128]{1,0:T(8,128)S(1)}, f32[16,128]{1,0:T(8,128)S(1)}, u32[]{:S(2)}, u32[]{:S(2)}) collective-permute-start(f32[16,128]{1,0:T(8,128)S(1)} %bitcast.226), channel_id=1, source_target_pairs={{0,4},{4,8},{8,12},{12,16},{16,20},{20,24},{24,28},{28,0},{1,5},{5... | collective-permute-start | bytes 24584 | tf_op jit(solution)/shard_map/ppermute | solution.py:18
  342.9 6.1 %collective-permute-start.7 = (f32[16,128]{1,0:T(8,128)S(1)}, f32[16,128]{1,0:T(8,128)S(1)}, u32[]{:S(2)}, u32[]{:S(2)}) collective-permute-start(f32[16,128]{1,0:T(8,128)S(1)} %bitcast.219), channel_id=1, source_target_pairs={{0,28},{4,0},{8,4},{12,8},{16,12},{20,16},{24,20},{28,24},{1,29},{... | collective-permute-start | bytes 24584 | tf_op jit(solution)/shard_map/ppermute | solution.py:18
  347.6 4.5 %collective-permute-start.6 = (f32[16,128]{1,0:T(8,128)S(1)}, f32[16,128]{1,0:T(8,128)S(1)}, u32[]{:S(2)}, u32[]{:S(2)}) collective-permute-start(f32[16,128]{1,0:T(8,128)S(1)} %bitcast.220), channel_id=1, source_target_pairs={{0,4},{4,8},{8,12},{12,16},{16,20},{20,24},{24,28},{28,0},{1,5},{5... | collective-permute-start | bytes 24584 | tf_op jit(solution)/shard_map/ppermute | solution.py:18
